TPU v7x, 32 devices: a whole 2x2x4 slice. The times are simulated.
32 devices in a mesh: cmp: 4 (over y, x), tgt: 8 (over z, core).
Axes of the slice: x: 2, y: 2, z: 4, core: 2. Of those that a mesh axis runs over, the one named last changes fastest.
Arguments:
- affinity: bfloat16 [8192, 12288], P('cmp', 'tgt'), may hold values from -6 to 6
- comp_vectors: bfloat16 [8192, 2048], P('cmp'), may hold values from -0.0625 to 0.0625
- targ_vectors: bfloat16 [12288, 2048], P('tgt'), may hold values from -0.0546875 to 0.0546875
- comp_values: float32 [2048], P('cmp'), may hold values from 0.05 to 4
- targ_values: float32 [2048], P('tgt'), may hold values from 0.05 to 4
Outputs:
- predicted: float32 [8192, 12288], P('cmp', 'tgt')
All inputs are finite; a program needn't handle non-finite values.
Results may differ from a plain program's by a relative error of at most 0.0037.
Values may be sent and summed in bfloat16 or wider, within the bound.
No kernel may reach another device: no remote copies, remote signals or barrier semaphores. Data moves between devices by JAX's collectives and lax.ppermute only.
A program may use at most 128 MiB of HBM per device.

v0:
```python
import jax
import jax.numpy as jnp
from jax import lax
from jax.sharding import PartitionSpec as P


def shards(affinity, comp_vectors, targ_vectors, comp_values, targ_values):
    vt_cols = targ_vectors
    half_t = lax.psum_scatter(
        lax.dot_general(
            vt_cols, affinity, (((0,), (1,)), ((), ())), preferred_element_type=jnp.float32
        ),
        "tgt",
        scatter_dimension=0,
        tiled=True,
    )
    comp_wide = comp_vectors.astype(jnp.float32)
    vc_cols = comp_wide
    coeffs = lax.psum_scatter(
        lax.dot_general(
            vc_cols,
            half_t,
            (((0,), (1,)), ((), ())),
            precision=lax.Precision.HIGHEST,
            preferred_element_type=jnp.float32,
        ),
        "cmp",
        scatter_dimension=0,
        tiled=True,
    )
    scaled = (coeffs / (comp_values[:, None] * targ_values[None, :] + 0.25)).astype(jnp.bfloat16)
    vc_cols = comp_vectors
    mapped = jnp.dot(
        vc_cols,
        lax.all_gather(scaled, "cmp", axis=0, tiled=True),
        preferred_element_type=jnp.float32,
    ).astype(jnp.bfloat16)
    vt_cols = targ_vectors
    return lax.dot_general(
        lax.all_gather(mapped, "tgt", axis=1, tiled=True),
        vt_cols,
        (((1,), (1,)), ((), ())),
        preferred_element_type=jnp.float32,
    )


def solution(mesh):
    in_specs = (P("cmp", "tgt"), P("cmp", None), P("tgt", None), P("cmp"), P("tgt"))
    out_specs = P("cmp", "tgt")
    return jax.shard_map(shards, mesh=mesh, in_specs=in_specs, out_specs=out_specs, check_vma=False)
```

profile of v0, /device:TPU:0, one launch (start us, length us, event | category | flops | bytes accessed | tf_op | source)
XLA Modules:
  0.0 386.2 jit_solution(5235248603564113408)
XLA Ops:
  6.5 0.0 reduce-scatter.3.cloned.1.call-start
  6.5 20.6 %fusion.1 = f32[2048,2048]{1,0:T(8,128)} fusion(bf16[1536,2048]{1,0:T(8,128)(2,1)} %param.7, bf16[2048,1536]{1,0:T(8,128)(2,1)} %param.5), kind=kOutput, calls=%fused_computation.4 | convolution fusion | flops 12884901888 | bytes 29360128 | tf_op jit(solution)/shard_map/dot_general | solution.py:10
  27.2 0.0 reduce-scatter.3.cloned.1.call-update
  27.2 0.0 copy-start
  27.2 0.0 copy-start.1
  27.2 0.0 reduce-scatter.5.cloned.1.call-start
  27.3 171.0 %reduce-scatter.3.cloned.1.call-done = f32[256,2048]{1,0:T(8,128)} async-done(((f32[2048,2048]{1,0:T(8,128)}), f32[256,2048]{1,0:T(8,128)}) %reduce-scatter.3.cloned.1.call-update) | async-done | bytes 2097168 | tf_op jit(solution)/shard_map/reduce_scatter | solution.py:9
  198.3 10.8 %convolution_bitcast_fusion = f32[2048,256]{0,1:T(8,128)} fusion(f32[256,2048]{1,0:T(8,128)} %reduce-scatter.3.cloned.1.call-done, bf16[2048,2048]{1,0:T(8,128)(2,1)} %param.6), kind=kOutput, calls=%fused_computation | convolution fusion | flops 12884901888 | bytes 12582912 | tf_op jit(solution)/shard_map/dot_general | solution.py:20
  209.0 0.0 reduce-scatter.5.cloned.1.call-update
  209.1 0.0 all-gather.3.cloned.1.call-start
  209.1 33.7 %reduce-scatter.5.cloned.1.call-done = f32[512,256]{0,1:T(8,128)} async-done(((f32[2048,256]{0,1:T(8,128)}), f32[512,256]{0,1:T(8,128)}) %reduce-scatter.5.cloned.1.call-update) | async-done | bytes 524304 | tf_op jit(solution)/shard_map/reduce_scatter | solution.py:19
  242.8 0.0 copy-done
  242.8 0.0 copy-done.1
  242.8 1.9 divide_convert_fusion
  244.7 0.0 all-gather.3.cloned.1.call-update
  244.7 0.2 all-gather.5.cloned.1.call-start
  244.9 26.4 %all-gather.3.cloned.1.call-done = bf16[2048,256]{0,1:T(8,128)(2,1)} async-done(((bf16[512,256]{0,1:T(8,128)(2,1)}), bf16[2048,256]{0,1:T(8,128)(2,1)}) %all-gather.3.cloned.1.call-update) | async-done | bytes 1048592 | tf_op jit(solution)/shard_map/all_gather | solution.py:35
  271.3 7.1 %fusion = bf16[2048,256]{0,1:T(8,128)(2,1)} fusion(bf16[2048,256]{0,1:T(8,128)(2,1)} %all-gather.3.cloned.1.call-done, bf16[2048,2048]{1,0:T(8,128)(2,1)} %param.6), kind=kOutput, calls=%fused_computation.2 | convolution fusion | flops 2148007936 | bytes 10485760 | tf_op jit(solution)/shard_map/dot_general | solution.py:33
  278.4 0.0 all-gather.5.cloned.1.call-update
  278.4 82.2 %all-gather.5.cloned.1.call-done = bf16[2048,2048]{0,1:T(8,128)(2,1)} async-done(((bf16[2048,256]{0,1:T(8,128)(2,1)}), bf16[2048,2048]{0,1:T(8,128)(2,1)}) %all-gather.5.cloned.1.call-update) | async-done | bytes 8388624 | tf_op jit(solution)/shard_map/all_gather | solution.py:40
  360.6 19.0 %fusion.2 = f32[2048,1536]{1,0:T(8,128)} fusion(bf16[2048,2048]{0,1:T(8,128)(2,1)} %all-gather.5.cloned.1.call-done, bf16[1536,2048]{1,0:T(8,128)(2,1)} %param.7), kind=kOutput, calls=%fused_computation.5 | convolution fusion | flops 12884901888 | bytes 27262976 | tf_op jit(solution)/shard_map/dot_general | solution.py:39
Async XLA Ops:
  6.5 191.7 %reduce-scatter.3.cloned.1.call-start = ((), (), s32[]{:S(2)}) async-start(), calls=%async_computation.2 | async-start | bytes 18874368 | tf_op jit(solution)/shard_map/reduce_scatter | solution.py:9
  27.2 215.6 %copy-start = (f32[512]{0:T(512)S(1)}, f32[512]{0:T(512)}, u32[]{:S(2)}) copy-start(f32[512]{0:T(512)} %param.8) | copy-start | bytes 6148
  27.2 215.6 %copy-start.1 = (f32[256]{0:T(256)S(1)}, f32[256]{0:T(256)}, u32[]{:S(2)}) copy-start(f32[256]{0:T(256)} %param.9) | copy-start | bytes 3076
  27.2 215.6 %reduce-scatter.5.cloned.1.call-start = ((), (), s32[]{:S(2)}) async-start(), calls=%async_computation.3 | async-start | bytes 2621440 | tf_op jit(solution)/shard_map/reduce_scatter | solution.py:19
  209.1 62.3 %all-gather.3.cloned.1.call-start = ((), (), s32[]{:S(2)}) async-start(), calls=%async_computation.4 | async-start | bytes 1310720 | tf_op jit(solution)/shard_map/all_gather | solution.py:35
  244.7 115.9 %all-gather.5.cloned.1.call-start = ((), (), s32[]{:S(2)}) async-start(), calls=%async_computation.5 | async-start | bytes 9437184 | tf_op jit(solution)/shard_map/all_gather | solution.py:40
Sparse Core Ops, SparseCore 0:
  27.3 170.9 reduce-scatter.2
  209.2 33.5 reduce-scatter.4
  244.8 26.4 all-gather.2
  278.5 82.0 all-gather.4
where the time goes:
time: 386 us
  waiting for transfers between devices  313 us (81%)
  matrix products  57.5 us (15%)
  between operations  13.1 us (3%)
    reduce_scatter x1, waiting for transfers between devices, shards(): lax.psum_scatter(lax.dot_general(vt_cols, affinity, (((0,), (1,)), ((), (...  171 us
    all_gather x1, waiting for transfers between devices, shards(): lax.all_gather(mapped, 'tgt', axis=1, tiled=True)  82.2 us
    reduce_scatter x1, waiting for transfers between devices, shards(): lax.psum_scatter(lax.dot_general(vc_cols, half_t, (((0,), (1,)), ((), ())...  33.7 us
    all_gather x1, waiting for transfers between devices, shards(): lax.all_gather(scaled, 'cmp', axis=0, tiled=True)  26.4 us
    dot_general x1, matrix products, shards(): lax.dot_general(vt_cols, affinity, (((0,), (1,)), ((), ())), preferred_el...  20.6 us
    dot_general x1, matrix products, shards(): lax.dot_general(lax.all_gather(mapped, 'tgt', axis=1, tiled=True), vt_col...  19 us
    dot_general x1, matrix products, shards(): lax.dot_general(vc_cols, half_t, (((0,), (1,)), ((), ())), precision=lax....  10.8 us
  transfers between devices with their start and end apart: 4, of which 4 were waited for; matrix products, arithmetic and copies ran while one was open for 0% of the time, Pallas kernels for 0%

commit v1 on v0

v1 whole, which is shorter than its diff:
```python
import functools

import jax
import jax.numpy as jnp
from jax import lax
from jax.experimental import pallas as pl
from jax.experimental.pallas import tpu as pltpu
from jax.sharding import PartitionSpec as P

F32, BF16, F16 = jnp.float32, jnp.bfloat16, jnp.float16
VMEM = 48 * 1024 * 1024
NT_DIMS = (((1,), (1,)), ((), ()))


def dot_nt(a, b):
    return lax.dot_general(a, b, NT_DIMS, preferred_element_type=F32)


def call(kernel, name, grid, idx, in_specs, args, out_spec, out_shape, scratch, flops, nbytes, aliases=None):
    return pl.pallas_call(
        kernel,
        name=name,
        out_shape=out_shape,
        grid_spec=pltpu.PrefetchScalarGridSpec(
            num_scalar_prefetch=1, grid=grid, in_specs=in_specs, out_specs=out_spec, scratch_shapes=scratch
        ),
        input_output_aliases=aliases or {},
        cost_estimate=pl.CostEstimate(flops=flops, bytes_accessed=nbytes, transcendentals=0),
        compiler_params=pltpu.CompilerParams(vmem_limit_bytes=VMEM),
    )(idx, *args)


def first_product(aff, vt, idx, k, chunks, width, add=None):
    rows, depth = aff.shape
    nq = idx.shape[0]
    tile = 256

    def kernel(s, y, *refs):
        vts, rest = refs[:nq], refs[nq:]
        out, wide = rest[-2:]

        @pl.when(pl.program_id(0) == 0)
        def _():
            for q in range(nq):
                wide[q * width : (q + 1) * width, :] = vts[q][...].T

        acc = dot_nt(wide[...], y[...])
        if add is not None:
            acc = acc + rest[0][...].astype(F32)
        out[...] = acc.astype(out.dtype)

    in_specs = [pl.BlockSpec((tile, depth), lambda i, s: (i, 0))]
    in_specs += [pl.BlockSpec((depth, width), functools.partial(lambda q, i, s: (0, s[q] * chunks + k), q)) for q in range(nq)]
    args = [aff] + [vt] * nq
    if add is not None:
        in_specs.append(pl.BlockSpec((nq * width, tile), lambda i, s: (0, i)))
        args.append(add)
    return call(
        kernel, "half", (rows // tile,), idx, in_specs, args,
        pl.BlockSpec((nq * width, tile), lambda i, s: (0, i)),
        jax.ShapeDtypeStruct((nq * width, rows), BF16),
        [pltpu.VMEM((nq * width, depth), BF16)],
        2 * rows * depth * nq * width, 2 * rows * depth + 2 * nq * width * (rows + depth),
    )


def second_product(half, vc, idx, block, scale, dtype):
    wide, rows = half.shape
    n = idx.shape[0]
    tile = min(256, block)
    sub = block // tile

    def kernel(s, h, v, out):
        acc = jnp.dot(h[...], v[...], preferred_element_type=F32)
        out[...] = (acc * scale).astype(out.dtype)

    return call(
        kernel, "coeffs", (n * sub,), idx,
        [
            pl.BlockSpec((wide, rows), lambda j, s: (0, 0)),
            pl.BlockSpec((rows, tile), lambda j, s: (0, s[j // sub] * sub + j % sub)),
        ],
        [half, vc],
        pl.BlockSpec((wide, tile), lambda j, s: (0, j)),
        jax.ShapeDtypeStruct((wide, n * block), dtype),
        [],
        2 * wide * rows * n * block, 2 * wide * rows + 2 * rows * n * block + 4 * wide * n * block,
    )


def third_product(vc, near, far, idx, block):
    rows, depth = vc.shape
    wide, cols = near.shape
    n = cols // block
    tile = 256

    def kernel(s, v, a, b, out):
        acc = jnp.zeros(out.shape, F32)
        for p in range(2 * n):
            piece = (a if p < n else b)[:, (p % n) * block : (p % n + 1) * block]
            acc += dot_nt(v[:, pl.ds(pl.multiple_of(s[p] * block, block), block)], piece)
        out[...] = acc.astype(out.dtype)

    return call(
        kernel, "mapped", (rows // tile,), idx,
        [
            pl.BlockSpec((tile, depth), lambda i, s: (i, 0)),
            pl.BlockSpec((wide, cols), lambda i, s: (0, 0)),
            pl.BlockSpec((wide, cols), lambda i, s: (0, 0)),
        ],
        [vc, near, far],
        pl.BlockSpec((tile, wide), lambda i, s: (i, 0)),
        jax.ShapeDtypeStruct((rows, wide), BF16),
        [],
        2 * rows * depth * wide, 2 * rows * depth + 2 * wide * depth + 2 * rows * wide,
    )


def last_product(own, other, vt, idx, k, block, width, before):
    rows, wide = own.shape
    depth = vt.shape[0]
    nq = idx.shape[0]
    tile = 256

    def kernel(s, m, r, v, *rest):
        out, cols, sems = rest[-3:]

        @pl.when(pl.program_id(0) == 0)
        def _():
            copies = []
            for q in range(nq):
                at = pl.multiple_of(s[q] * block + k * width, width)
                copies.append(pltpu.make_async_copy(v.at[:, pl.ds(at, width)], cols.at[:, pl.ds(q * width, width)], sems.at[q]))
            for copy in copies:
                copy.start()
            for copy in copies:
                copy.wait()

        acc = dot_nt(jnp.concatenate([m[...], r[...]], axis=1), cols[...])
        if before is not None:
            acc = acc + rest[0][...]
        out[...] = acc

    in_specs = [
        pl.BlockSpec((tile, wide), lambda i, s: (i, 0)),
        pl.BlockSpec((tile, wide), lambda i, s: (i, 0)),
        pl.BlockSpec(memory_space=pl.ANY),
    ]
    args = [own, other, vt]
    aliases = None
    if before is not None:
        in_specs.append(pl.BlockSpec((tile, depth), lambda i, s: (i, 0)))
        args.append(before)
        aliases = {4: 0}
    return call(
        kernel, "predicted", (rows // tile,), idx, in_specs, args,
        pl.BlockSpec((tile, depth), lambda i, s: (i, 0)),
        jax.ShapeDtypeStruct((rows, depth), F32),
        [pltpu.VMEM((depth, 2 * wide), BF16), pltpu.SemaphoreType.DMA((nq,))],
        4 * rows * depth * wide, 4 * rows * wide + 4 * rows * depth * (1 if before is None else 2) + 4 * depth * wide,
        aliases,
    )


def shards(nc, nt, affinity, comp_vectors, targ_vectors, comp_values, targ_values):
    cbits, tbits = nc.bit_length() - 1, nt.bit_length() - 2
    orders = (list(range(cbits)), list(reversed(range(cbits))))
    iblock, jblock = comp_vectors.shape[1] // nc, targ_vectors.shape[1] // nt
    chunks = 2 if jblock % 256 == 0 else 1
    width = jblock // chunks
    at_c, at_t = lax.axis_index("cmp"), lax.axis_index("tgt")

    def offset(position, order):
        return sum(((position >> (len(order) - 1 - t)) & 1) << bit for t, bit in enumerate(order))

    even = jnp.array([offset(p, orders[0]) for p in range(nc)], jnp.int32)
    odd = jnp.array([offset(p, orders[1]) for p in range(nc)], jnp.int32)
    c_blocks = jnp.where(at_t % 2 == 0, even, odd) ^ at_c
    keep = jnp.array([offset(q, range(1, tbits + 1)) for q in range(nt // 2)], jnp.int32) ^ at_t
    give = keep ^ 1

    def swap_c(x, t):
        pairs = [(c * nt + i, (c ^ (1 << orders[i % 2][t])) * nt + i) for c in range(nc) for i in range(nt)]
        return lax.ppermute(x, ("cmp", "tgt"), pairs)

    def swap_t(x, bit):
        return lax.ppermute(x, "tgt", [(i, i ^ (1 << bit)) for i in range(nt)])

    bound = 6 * 0.0625 * 0.0546875 * affinity.shape[0] * nc * affinity.shape[1] * nt
    scale = 1.0
    while bound * scale > 65000:
        scale *= 0.5

    sent = [first_product(affinity, targ_vectors, give, k, chunks, width) for k in range(chunks)]
    came = [swap_t(x, 0) for x in sent]
    out = None
    pieces = []
    for k in range(chunks):
        half = first_product(affinity, targ_vectors, keep, k, chunks, width, came[k])
        far = swap_c(second_product(half, comp_vectors, c_blocks[nc // 2 :], iblock, scale, F32).astype(F16), 0)
        near = second_product(half, comp_vectors, c_blocks[: nc // 2], iblock, scale, F32)
        pieces.append((near, far))
    scaled = []
    for k in range(chunks):
        near, far = pieces[k]
        total = near + far.astype(F32)
        for t in range(1, cbits):
            n = total.shape[1] // 2
            total = total[:, :n] + swap_c(total[:, n:].astype(F16), t).astype(F32)
        for t in range(tbits):
            n = total.shape[0] // 2
            total = total[:n] + swap_t(total[n:].astype(F16), 1 + t).astype(F32)
        lt = targ_values[k * width : (k + 1) * width]
        scaled.append((total * (1 / scale) / (lt[:, None] * comp_values[None, :] + 0.25)).astype(BF16))
    for k in range(chunks):
        part = scaled[k]
        for t in reversed(range(tbits)):
            part = jnp.concatenate([part, swap_t(part, 1 + t)], axis=0)
        for t in reversed(range(1, cbits)):
            part = jnp.concatenate([part, swap_c(part, t)], axis=1)
        own = third_product(comp_vectors, part, swap_c(part, 0), c_blocks, iblock)
        other = swap_t(own, 0)
        out = last_product(own, other, targ_vectors, jnp.concatenate([keep, give]), k, jblock, width, out)
    return out


def solution(mesh):
    in_specs = (P("cmp", "tgt"), P("cmp", None), P("tgt", None), P("cmp"), P("tgt"))
    out_specs = P("cmp", "tgt")
    body = functools.partial(shards, mesh.shape["cmp"], mesh.shape["tgt"])
    return jax.shard_map(body, mesh=mesh, in_specs=in_specs, out_specs=out_specs, check_vma=False)
```

time: 386 us -> 202 us (0.52)
  waiting for transfers between devices: 313 us -> 62.5 us
  Pallas kernels: 0 us -> 110 us
  matrix products: 57.5 us -> 0 us
  starting transfers between devices: 0.31 us -> 24.5 us
  between operations: 13.1 us -> 0.33 us
    reduce_scatter x2 -> x0, waiting for transfers between devices: 205 us -> none  [the longest x1 171 us: shards(): lax.psum_scatter(lax.dot_general(vt_cols, affinity, (((0,), (1,)), ((), (...]
    pallas_call x0 -> x12, Pallas kernels: none -> 110 us  [call(): pl.pallas_call(kernel, name=name, out_shape=out_shape, grid_spec=pltpu.Pr...]
    all_gather x2 -> x0, waiting for transfers between devices: 109 us -> none  [the longest x1 82.2 us: shards(): lax.all_gather(mapped, 'tgt', axis=1, tiled=True)]
    ppermute x0 -> x20, waiting for transfers between devices: none -> 62.5 us  [the longest x12 32 us: swap_t(): return lax.ppermute(x, 'tgt', [(i, i ^ 1 << bit) for i in range(nt)])]
    dot_general x4 -> x0, matrix products: 57.5 us -> none  [the longest x1 20.6 us: shards(): lax.dot_general(vt_cols, affinity, (((0,), (1,)), ((), ())), preferred_el...]
    ppermute x0 -> x20, starting transfers between devices: none -> 24.5 us  [the longest x8 12.5 us: swap_c(): return lax.ppermute(x, ('cmp', 'tgt'), pairs)]
  transfers between devices with their start and end apart: 4 -> 20, of which waited for: 4 -> 13; matrix products, arithmetic and copies ran while one was open for 0% -> 1% of each run, Pallas kernels for 0% -> 41%
where the time goes in v1:
time: 202 us; the launch traced here: 201 us
  Pallas kernels  110 us (54%)
  waiting for transfers between devices  62.5 us (31%)
  starting transfers between devices  24.5 us (12%)
  other arithmetic  3.49 us (2%)
    pallas_call x12, Pallas kernels, call(): pl.pallas_call(kernel, name=name, out_shape=out_shape, grid_spec=pltpu.Pr...  110 us
    ppermute x12, waiting for transfers between devices, swap_t(): return lax.ppermute(x, 'tgt', [(i, i ^ 1 << bit) for i in range(nt)])  32 us
    ppermute x8, waiting for transfers between devices, swap_c(): return lax.ppermute(x, ('cmp', 'tgt'), pairs)  30.5 us
    ppermute x8, starting transfers between devices, swap_c(): return lax.ppermute(x, ('cmp', 'tgt'), pairs)  12.5 us
    ppermute x12, starting transfers between devices, swap_t(): return lax.ppermute(x, 'tgt', [(i, i ^ 1 << bit) for i in range(nt)])  12 us
  transfers between devices with their start and end apart: 20, of which 13 were waited for; matrix products, arithmetic and copies ran while one was open for 1% of the time, Pallas kernels for 41%

profile of v1, /device:TPU:0, one launch (start us, length us, event | category | flops | bytes accessed | tf_op | source)
XLA Modules:
  0.0 200.7 jit_solution(17903415651997754610)
XLA Ops:
  0.0 0.7 broadcast_xor_fusion.1
  0.7 10.4 %half.4 = bf16[512,2048]{1,0:T(8,128)(2,1)} custom-call(s32[4]{0:T(128)S(1)} %get-tuple-element.12.s, bf16[2048,1536]{1,0:T(8,128)(2,1)} %y.7, bf16[1536,2048]{1,0:T(8,128)(2,1)} %v.15, bf16[1536,2048]{1,0:T(8,128)(2,1)} %v.15, bf16[1536,2048]{1,0:T(8,128)(2,1)} %v.15, bf16[1536,2048]{1,0:T(8,128)(2,1)} %v.15), custom_call_target="tpu_custom_call" | custom-call | flops 3221225472 | bytes 9961472 | tf_op jit(solution)/shard_map/half/pallas_call | solution.py:20
  11.0 0.5 collective-permute-start
  11.5 10.3 %half.6 = bf16[512,2048]{1,0:T(8,128)(2,1)} custom-call(s32[4]{0:T(128)S(1)} %get-tuple-element.12.s, bf16[2048,1536]{1,0:T(8,128)(2,1)} %y.7, bf16[1536,2048]{1,0:T(8,128)(2,1)} %v.15, bf16[1536,2048]{1,0:T(8,128)(2,1)} %v.15, bf16[1536,2048]{1,0:T(8,128)(2,1)} %v.15, bf16[1536,2048]{1,0:T(8,128)(2,1)} %v.15), custom_call_target="tpu_custom_call" | custom-call | flops 3221225472 | bytes 9961472 | tf_op jit(solution)/shard_map/half/pallas_call | solution.py:20
  21.8 0.0 collective-permute-start.10
  21.9 0.1 fusion.8
  22.0 9.8 %half.5.h = bf16[512,2048]{1,0:T(8,128)(2,1)S(1)} custom-call(s32[4]{0:T(128)S(1)} %get-tuple-element.11.s, bf16[2048,1536]{1,0:T(8,128)(2,1)} %y.7, bf16[1536,2048]{1,0:T(8,128)(2,1)} %v.15, bf16[1536,2048]{1,0:T(8,128)(2,1)} %v.15, bf16[1536,2048]{1,0:T(8,128)(2,1)} %v.15, bf16[1536,2048]{1,0:T(8,128)(2,1)} %v.15, ...), custom_call_target="tpu_custom_call" | custom-call | flops 3221225472 | bytes 9961472 | tf_op jit(solution)/shard_map/half/pallas_call | solution.py:20
  31.7 5.4 %coeffs.5 = f32[512,1024]{1,0:T(8,128)S(1)} custom-call(s32[2]{0:T(128)S(1)} %get-tuple-element.9.s, bf16[512,2048]{1,0:T(8,128)(2,1)S(1)} %half.5.h, bf16[2048,2048]{1,0:T(8,128)(2,1)} %v.13), custom_call_target="tpu_custom_call" | custom-call | flops 2147483648 | bytes 8388608 | tf_op jit(solution)/shard_map/coeffs/pallas_call | solution.py:20
  37.2 0.2 convert_element_type.42
  37.4 3.1 %collective-permute-start.1 = (f16[512,1024]{1,0:T(8,128)(2,1)S(1)}, f16[512,1024]{1,0:T(8,128)(2,1)S(1)}, u32[]{:S(2)}, u32[]{:S(2)}) collective-permute-start(f16[512,1024]{1,0:T(8,128)(2,1)S(1)} %convert_element_type.42), channel_id=1, source_target_pairs={{0,8},{1,17},{2,10},{3,19},{4,12},{5,21},{6,14},{7,23},{8,0},{9,25... | collective-permute-start | bytes 3145736 | tf_op jit(solution)/shard_map/ppermute | solution.py:184
  40.4 0.0 collective-permute-done.10.refs_4_
  40.4 9.5 %half.7.h = bf16[512,2048]{1,0:T(8,128)(2,1)S(1)} custom-call(s32[4]{0:T(128)S(1)} %get-tuple-element.11.s, bf16[2048,1536]{1,0:T(8,128)(2,1)} %y.7, bf16[1536,2048]{1,0:T(8,128)(2,1)} %v.15, bf16[1536,2048]{1,0:T(8,128)(2,1)} %v.15, bf16[1536,2048]{1,0:T(8,128)(2,1)} %v.15, bf16[1536,2048]{1,0:T(8,128)(2,1)} %v.15, ...), custom_call_target="tpu_custom_call" | custom-call | flops 3221225472 | bytes 9961472 | tf_op jit(solution)/shard_map/half/pallas_call | solution.py:20
  50.0 5.4 %coeffs.7 = f32[512,1024]{1,0:T(8,128)S(1)} custom-call(s32[2]{0:T(128)S(1)} %get-tuple-element.9.s, bf16[512,2048]{1,0:T(8,128)(2,1)S(1)} %half.7.h, bf16[2048,2048]{1,0:T(8,128)(2,1)} %v.13), custom_call_target="tpu_custom_call" | custom-call | flops 2147483648 | bytes 8388608 | tf_op jit(solution)/shard_map/coeffs/pallas_call | solution.py:20
  55.4 0.2 convert_element_type.48
  55.6 0.1 collective-permute-start.11
  55.6 5.4 %coeffs.4 = f32[512,1024]{1,0:T(8,128)S(1)} custom-call(s32[2]{0:T(128)S(1)} %get-tuple-element.10.s, bf16[512,2048]{1,0:T(8,128)(2,1)S(1)} %half.5.h, bf16[2048,2048]{1,0:T(8,128)(2,1)} %v.13), custom_call_target="tpu_custom_call" | custom-call | flops 2147483648 | bytes 8388608 | tf_op jit(solution)/shard_map/coeffs/pallas_call | solution.py:20
  61.1 5.4 %coeffs.6 = f32[512,1024]{1,0:T(8,128)S(1)} custom-call(s32[2]{0:T(128)S(1)} %get-tuple-element.10.s, bf16[512,2048]{1,0:T(8,128)(2,1)S(1)} %half.7.h, bf16[2048,2048]{1,0:T(8,128)(2,1)} %v.13), custom_call_target="tpu_custom_call" | custom-call | flops 2147483648 | bytes 8388608 | tf_op jit(solution)/shard_map/coeffs/pallas_call | solution.py:20
  66.5 0.5 convert_add_fusion.1
  67.0 0.1 slice_convert_fusion.1
  67.1 2.0 %collective-permute-start.2 = (f16[512,512]{1,0:T(8,128)(2,1)S(1)}, f16[512,512]{1,0:T(8,128)(2,1)S(1)}, u32[]{:S(2)}, u32[]{:S(2)}) collective-permute-start(f16[512,512]{1,0:T(8,128)(2,1)S(1)} %slice_convert_fusion.1), channel_id=1, source_target_pairs={{0,16},{1,9},{2,18},{3,11},{4,20},{5,13},{6,22},{7,15},{8,24},{9,1... | collective-permute-start | bytes 1572872 | tf_op jit(solution)/shard_map/ppermute | solution.py:184
  69.1 2.1 %collective-permute-done.11 = f16[512,1024]{1,0:T(8,128)(2,1)S(1)} collective-permute-done((f16[512,1024]{1,0:T(8,128)(2,1)S(1)}, f16[512,1024]{1,0:T(8,128)(2,1)S(1)}, u32[]{:S(2)}, u32[]{:S(2)}) %collective-permute-start.11) | collective-permute-done | bytes 1048608 | tf_op jit(solution)/shard_map/ppermute | solution.py:184
  71.3 0.5 convert_add_fusion
  71.8 0.1 slice_convert_fusion
  71.9 1.3 collective-permute-start.12
  73.2 3.1 %collective-permute-done.2 = f16[512,512]{1,0:T(8,128)(2,1)S(1)} collective-permute-done((f16[512,512]{1,0:T(8,128)(2,1)S(1)}, f16[512,512]{1,0:T(8,128)(2,1)S(1)}, u32[]{:S(2)}, u32[]{:S(2)}) %collective-permute-start.2) | collective-permute-done | bytes 524320 | tf_op jit(solution)/shard_map/ppermute | solution.py:184
  76.3 0.2 slice_add_fusion.1
  76.6 2.1 %collective-permute-start.3 = (f16[256,512]{1,0:T(8,128)(2,1)S(1)}, f16[256,512]{1,0:T(8,128)(2,1)S(1)}, u32[]{:S(2)}, u32[]{:S(2)}) collective-permute-start(f16[256,512]{1,0:T(8,128)(2,1)S(1)} %slice_convert_fusion.3), channel_id=1, source_target_pairs={{0,2},{1,3},{2,0},{3,1},{4,6},{5,7},{6,4},{7,5},{8,10},{9,11},{10,... | collective-permute-start | bytes 786440 | tf_op jit(solution)/shard_map/ppermute | solution.py:187
  78.7 3.3 %collective-permute-done.12 = f16[512,512]{1,0:T(8,128)(2,1)S(1)} collective-permute-done((f16[512,512]{1,0:T(8,128)(2,1)S(1)}, f16[512,512]{1,0:T(8,128)(2,1)S(1)}, u32[]{:S(2)}, u32[]{:S(2)}) %collective-permute-start.12) | collective-permute-done | bytes 524320 | tf_op jit(solution)/shard_map/ppermute | solution.py:184
  81.9 0.2 slice_add_fusion
  82.1 0.0 copy-start.1
  82.1 0.0 copy-start
  82.2 2.1 %collective-permute-start.13 = (f16[256,512]{1,0:T(8,128)(2,1)S(1)}, f16[256,512]{1,0:T(8,128)(2,1)S(1)}, u32[]{:S(2)}, u32[]{:S(2)}) collective-permute-start(f16[256,512]{1,0:T(8,128)(2,1)S(1)} %slice_convert_fusion.2), channel_id=1, source_target_pairs={{0,2},{1,3},{2,0},{3,1},{4,6},{5,7},{6,4},{7,5},{8,10},{9,11},{10,... | collective-permute-start | bytes 786440 | tf_op jit(solution)/shard_map/ppermute | solution.py:187
  84.3 0.4 collective-permute-done.3
  84.7 0.1 slice_add_fusion.3
  84.8 2.6 %collective-permute-start.4 = (f16[128,512]{1,0:T(8,128)(2,1)S(1)}, f16[128,512]{1,0:T(8,128)(2,1)S(1)}, u32[]{:S(2)}, u32[]{:S(2)}) collective-permute-start(f16[128,512]{1,0:T(8,128)(2,1)S(1)} %slice_convert_fusion.5), channel_id=1, source_target_pairs={{0,4},{1,5},{2,6},{3,7},{4,0},{5,1},{6,2},{7,3},{8,12},{9,13},{10,... | collective-permute-start | bytes 393224 | tf_op jit(solution)/shard_map/ppermute | solution.py:187
  87.4 5.7 %collective-permute-done.13 = f16[256,512]{1,0:T(8,128)(2,1)S(1)} collective-permute-done((f16[256,512]{1,0:T(8,128)(2,1)S(1)}, f16[256,512]{1,0:T(8,128)(2,1)S(1)}, u32[]{:S(2)}, u32[]{:S(2)}) %collective-permute-start.13) | collective-permute-done | bytes 262176 | tf_op jit(solution)/shard_map/ppermute | solution.py:187
  93.1 0.1 slice_add_fusion.2
  93.2 1.6 collective-permute-start.14
  94.9 7.5 %collective-permute-done.14 = f16[128,512]{1,0:T(8,128)(2,1)S(1)} collective-permute-done((f16[128,512]{1,0:T(8,128)(2,1)S(1)}, f16[128,512]{1,0:T(8,128)(2,1)S(1)}, u32[]{:S(2)}, u32[]{:S(2)}) %collective-permute-start.14) | collective-permute-done | bytes 131104 | tf_op jit(solution)/shard_map/ppermute | solution.py:187
  102.4 0.2 fusion.5
  102.6 0.1 collective-permute-start.15
  102.6 5.9 %collective-permute-done.15 = bf16[128,512]{1,0:T(8,128)(2,1)S(1)} collective-permute-done((bf16[128,512]{1,0:T(8,128)(2,1)S(1)}, bf16[128,512]{1,0:T(8,128)(2,1)S(1)}, u32[]{:S(2)}, u32[]{:S(2)}) %collective-permute-start.15) | collective-permute-done | bytes 131104 | tf_op jit(solution)/shard_map/ppermute | solution.py:187
  108.5 0.1 collective-permute-start.16
  108.6 2.7 %collective-permute-start.5 = (bf16[128,512]{1,0:T(8,128)(2,1)S(1)}, bf16[128,512]{1,0:T(8,128)(2,1)S(1)}, u32[]{:S(2)}, u32[]{:S(2)}) collective-permute-start(bf16[128,512]{1,0:T(8,128)(2,1)S(1)} %get-tuple-element.6), channel_id=1, source_target_pairs={{0,4},{1,5},{2,6},{3,7},{4,0},{5,1},{6,2},{7,3},{8,12},{9,13},{10,... | collective-permute-start | bytes 393224 | tf_op jit(solution)/shard_map/ppermute | solution.py:187
  111.3 6.2 %collective-permute-done.16 = bf16[256,512]{1,0:T(8,128)(2,1)S(1)} collective-permute-done((bf16[256,512]{1,0:T(8,128)(2,1)S(1)}, bf16[256,512]{1,0:T(8,128)(2,1)S(1)}, u32[]{:S(2)}, u32[]{:S(2)}) %collective-permute-start.16) | collective-permute-done | bytes 262176 | tf_op jit(solution)/shard_map/ppermute | solution.py:187
  117.5 5.7 %collective-permute-start.17 = (bf16[512,512]{1,0:T(8,128)(2,1)S(1)}, bf16[512,512]{1,0:T(8,128)(2,1)S(1)}, u32[]{:S(2)}, u32[]{:S(2)}) collective-permute-start(bf16[512,512]{1,0:T(8,128)(2,1)S(1)} %pad_maximum_fusion.3), channel_id=1, source_target_pairs={{0,16},{1,9},{2,18},{3,11},{4,20},{5,13},{6,22},{7,15},{8,24},{9,1... | collective-permute-start | bytes 1572872 | tf_op jit(solution)/shard_map/ppermute | solution.py:184
  123.3 0.1 collective-permute-start.6
  123.4 6.4 %collective-permute-done.6 = bf16[256,512]{1,0:T(8,128)(2,1)S(1)} collective-permute-done((bf16[256,512]{1,0:T(8,128)(2,1)S(1)}, bf16[256,512]{1,0:T(8,128)(2,1)S(1)}, u32[]{:S(2)}, u32[]{:S(2)}) %collective-permute-start.6) | collective-permute-done | bytes 262176 | tf_op jit(solution)/shard_map/ppermute | solution.py:187
  129.8 0.1 collective-permute-start.7
  129.8 5.7 %collective-permute-done.17 = bf16[512,512]{1,0:T(8,128)(2,1)S(1)} collective-permute-done((bf16[512,512]{1,0:T(8,128)(2,1)S(1)}, bf16[512,512]{1,0:T(8,128)(2,1)S(1)}, u32[]{:S(2)}, u32[]{:S(2)}) %collective-permute-start.17) | collective-permute-done | bytes 524320 | tf_op jit(solution)/shard_map/ppermute | solution.py:184
  135.5 0.1 pad_maximum_fusion.1.a
  135.7 0.1 collective-permute-start.18
  135.8 11.0 %collective-permute-done.7 = bf16[512,512]{1,0:T(8,128)(2,1)S(1)} collective-permute-done((bf16[512,512]{1,0:T(8,128)(2,1)S(1)}, bf16[512,512]{1,0:T(8,128)(2,1)S(1)}, u32[]{:S(2)}, u32[]{:S(2)}) %collective-permute-start.7) | collective-permute-done | bytes 524320 | tf_op jit(solution)/shard_map/ppermute | solution.py:184
  146.8 0.1 pad_maximum_fusion.a
  146.9 0.1 collective-permute-start.8
  147.0 3.5 %collective-permute-done.18.b = bf16[512,1024]{1,0:T(8,128)(2,1)S(1)} collective-permute-done((bf16[512,1024]{1,0:T(8,128)(2,1)S(1)}, bf16[512,1024]{1,0:T(8,128)(2,1)S(1)}, u32[]{:S(2)}, u32[]{:S(2)}) %collective-permute-start.18) | collective-permute-done | bytes 1048608 | tf_op jit(solution)/shard_map/ppermute | solution.py:184
  150.5 9.5 %mapped.3.m = bf16[2048,512]{1,0:T(8,128)(2,1)S(1)} custom-call(s32[4]{0:T(128)S(1)} %fusion.6.s, bf16[2048,2048]{1,0:T(8,128)(2,1)} %v.13, bf16[512,1024]{1,0:T(8,128)(2,1)S(1)} %pad_maximum_fusion.1.a, bf16[512,1024]{1,0:T(8,128)(2,1)S(1)} %collective-permute-done.18.b), custom_call_target="tpu_custom_call" | custom-call | flops 4294967296 | bytes 12582912 | tf_op jit(solution)/shard_map/mapped/pallas_call | solution.py:20
  160.0 0.1 collective-permute-start.19
  160.1 1.7 collective-permute-done.8.b
  161.8 9.5 %mapped.2.m = bf16[2048,512]{1,0:T(8,128)(2,1)S(1)} custom-call(s32[4]{0:T(128)S(1)} %fusion.6.s, bf16[2048,2048]{1,0:T(8,128)(2,1)} %v.13, bf16[512,1024]{1,0:T(8,128)(2,1)S(1)} %pad_maximum_fusion.a, bf16[512,1024]{1,0:T(8,128)(2,1)S(1)} %collective-permute-done.8.b), custom_call_target="tpu_custom_call" | custom-call | flops 4294967296 | bytes 12582912 | tf_op jit(solution)/shard_map/mapped/pallas_call | solution.py:20
  171.2 0.1 collective-permute-start.9
  171.3 0.1 pad_add_fusion.s
  171.4 12.4 %predicted.2.rest_0_ = f32[2048,1536]{1,0:T(8,128)} custom-call(s32[8]{0:T(128)S(1)} %pad_add_fusion.s, bf16[2048,512]{1,0:T(8,128)(2,1)S(1)} %mapped.3.m, bf16[2048,512]{1,0:T(8,128)(2,1)S(1)} %collective-permute-done.19.r, bf16[1536,2048]{1,0:T(8,128)(2,1)} %v.15), custom_call_target="tpu_custom_call" | custom-call | flops 6442450944 | bytes 19922944 | tf_op jit(solution)/shard_map/predicted/pallas_call | solution.py:20
  183.8 16.9 %predicted.3 = f32[2048,1536]{1,0:T(8,128)} custom-call(s32[8]{0:T(128)S(1)} %pad_add_fusion.s, bf16[2048,512]{1,0:T(8,128)(2,1)S(1)} %mapped.2.m, bf16[2048,512]{1,0:T(8,128)(2,1)S(1)} %collective-permute-done.9.r, bf16[1536,2048]{1,0:T(8,128)(2,1)} %v.15, f32[2048,1536]{1,0:T(8,128)} %predicted.2.rest_0_), custom_call_target="tpu_custom_call", output_to_operand_aliasing={{}: (4, {})} | custom-call | flops 6442450944 | bytes 32505856 | tf_op jit(solution)/shard_map/predicted/pallas_call | solution.py:20
  (20 shorter events, 0.3 us)
Async XLA Ops:
  11.0 10.8 %copy-start.2 = (s32[4]{0:T(128)S(1)}, s32[4]{0:T(128)}, u32[]{:S(2)}) copy-start(s32[4]{0:T(128)} %constant.33.clone) | copy-start | bytes 52
  11.0 10.9 %collective-permute-start = (bf16[512,2048]{1,0:T(8,128)(2,1)}, bf16[512,2048]{1,0:T(8,128)(2,1)}, u32[]{:S(2)}, u32[]{:S(2)}) collective-permute-start(bf16[512,2048]{1,0:T(8,128)(2,1)} %half.4), channel_id=1, source_target_pairs={{0,1},{1,0},{2,3},{3,2},{4,5},{5,4},{6,7},{7,6},{8,9},{9,8},{10,11... | collective-permute-start | bytes 6291464 | tf_op jit(solution)/shard_map/ppermute | solution.py:187
  21.8 18.6 %collective-permute-start.10 = (bf16[512,2048]{1,0:T(8,128)(2,1)}, bf16[512,2048]{1,0:T(8,128)(2,1)S(1)}, u32[]{:S(2)}, u32[]{:S(2)}) collective-permute-start(bf16[512,2048]{1,0:T(8,128)(2,1)} %half.6), channel_id=1, source_target_pairs={{0,1},{1,0},{2,3},{3,2},{4,5},{5,4},{6,7},{7,6},{8,9},{9,8},{10,11... | collective-permute-start | bytes 6291464 | tf_op jit(solution)/shard_map/ppermute | solution.py:187
  37.4 29.1 %collective-permute-start.1 = (f16[512,1024]{1,0:T(8,128)(2,1)S(1)}, f16[512,1024]{1,0:T(8,128)(2,1)S(1)}, u32[]{:S(2)}, u32[]{:S(2)}) collective-permute-start(f16[512,1024]{1,0:T(8,128)(2,1)S(1)} %convert_element_type.42), channel_id=1, source_target_pairs={{0,8},{1,17},{2,10},{3,19},{4,12},{5,21},{6,14},{7,23},{8,0},{9,25... | collective-permute-start | bytes 3145736 | tf_op jit(solution)/shard_map/ppermute | solution.py:184
  55.6 15.7 %collective-permute-start.11 = (f16[512,1024]{1,0:T(8,128)(2,1)S(1)}, f16[512,1024]{1,0:T(8,128)(2,1)S(1)}, u32[]{:S(2)}, u32[]{:S(2)}) collective-permute-start(f16[512,1024]{1,0:T(8,128)(2,1)S(1)} %convert_element_type.48), channel_id=1, source_target_pairs={{0,8},{1,17},{2,10},{3,19},{4,12},{5,21},{6,14},{7,23},{8,0},{9,25... | collective-permute-start | bytes 3145736 | tf_op jit(solution)/shard_map/ppermute | solution.py:184
  67.1 9.2 %collective-permute-start.2 = (f16[512,512]{1,0:T(8,128)(2,1)S(1)}, f16[512,512]{1,0:T(8,128)(2,1)S(1)}, u32[]{:S(2)}, u32[]{:S(2)}) collective-permute-start(f16[512,512]{1,0:T(8,128)(2,1)S(1)} %slice_convert_fusion.1), channel_id=1, source_target_pairs={{0,16},{1,9},{2,18},{3,11},{4,20},{5,13},{6,22},{7,15},{8,24},{9,1... | collective-permute-start | bytes 1572872 | tf_op jit(solution)/shard_map/ppermute | solution.py:184
  71.9 10.1 %collective-permute-start.12 = (f16[512,512]{1,0:T(8,128)(2,1)S(1)}, f16[512,512]{1,0:T(8,128)(2,1)S(1)}, u32[]{:S(2)}, u32[]{:S(2)}) collective-permute-start(f16[512,512]{1,0:T(8,128)(2,1)S(1)} %slice_convert_fusion), channel_id=1, source_target_pairs={{0,16},{1,9},{2,18},{3,11},{4,20},{5,13},{6,22},{7,15},{8,24},{9,1... | collective-permute-start | bytes 1572872 | tf_op jit(solution)/shard_map/ppermute | solution.py:184
  76.6 8.1 %collective-permute-start.3 = (f16[256,512]{1,0:T(8,128)(2,1)S(1)}, f16[256,512]{1,0:T(8,128)(2,1)S(1)}, u32[]{:S(2)}, u32[]{:S(2)}) collective-permute-start(f16[256,512]{1,0:T(8,128)(2,1)S(1)} %slice_convert_fusion.3), channel_id=1, source_target_pairs={{0,2},{1,3},{2,0},{3,1},{4,6},{5,7},{6,4},{7,5},{8,10},{9,11},{10,... | collective-permute-start | bytes 786440 | tf_op jit(solution)/shard_map/ppermute | solution.py:187
  82.1 12.7 %copy-start.1 = (f32[256]{0:T(256)S(1)}, f32[256]{0:T(256)}, u32[]{:S(2)}) copy-start(f32[256]{0:T(256)} %param.12) | copy-start | bytes 3076
  82.1 20.2 %copy-start = (f32[512]{0:T(512)S(1)}, f32[512]{0:T(512)}, u32[]{:S(2)}) copy-start(f32[512]{0:T(512)} %param.11) | copy-start | bytes 6148
  82.2 10.9 %collective-permute-start.13 = (f16[256,512]{1,0:T(8,128)(2,1)S(1)}, f16[256,512]{1,0:T(8,128)(2,1)S(1)}, u32[]{:S(2)}, u32[]{:S(2)}) collective-permute-start(f16[256,512]{1,0:T(8,128)(2,1)S(1)} %slice_convert_fusion.2), channel_id=1, source_target_pairs={{0,2},{1,3},{2,0},{3,1},{4,6},{5,7},{6,4},{7,5},{8,10},{9,11},{10,... | collective-permute-start | bytes 786440 | tf_op jit(solution)/shard_map/ppermute | solution.py:187
  84.8 10.1 %collective-permute-start.4 = (f16[128,512]{1,0:T(8,128)(2,1)S(1)}, f16[128,512]{1,0:T(8,128)(2,1)S(1)}, u32[]{:S(2)}, u32[]{:S(2)}) collective-permute-start(f16[128,512]{1,0:T(8,128)(2,1)S(1)} %slice_convert_fusion.5), channel_id=1, source_target_pairs={{0,4},{1,5},{2,6},{3,7},{4,0},{5,1},{6,2},{7,3},{8,12},{9,13},{10,... | collective-permute-start | bytes 393224 | tf_op jit(solution)/shard_map/ppermute | solution.py:187
  93.2 9.1 %collective-permute-start.14 = (f16[128,512]{1,0:T(8,128)(2,1)S(1)}, f16[128,512]{1,0:T(8,128)(2,1)S(1)}, u32[]{:S(2)}, u32[]{:S(2)}) collective-permute-start(f16[128,512]{1,0:T(8,128)(2,1)S(1)} %slice_convert_fusion.4), channel_id=1, source_target_pairs={{0,4},{1,5},{2,6},{3,7},{4,0},{5,1},{6,2},{7,3},{8,12},{9,13},{10,... | collective-permute-start | bytes 393224 | tf_op jit(solution)/shard_map/ppermute | solution.py:187
  102.6 5.9 %collective-permute-start.15 = (bf16[128,512]{1,0:T(8,128)(2,1)S(1)}, bf16[128,512]{1,0:T(8,128)(2,1)S(1)}, u32[]{:S(2)}, u32[]{:S(2)}) collective-permute-start(bf16[128,512]{1,0:T(8,128)(2,1)S(1)} %get-tuple-element.5), channel_id=1, source_target_pairs={{0,4},{1,5},{2,6},{3,7},{4,0},{5,1},{6,2},{7,3},{8,12},{9,13},{10,... | collective-permute-start | bytes 393224 | tf_op jit(solution)/shard_map/ppermute | solution.py:187
  108.5 9.0 %collective-permute-start.16 = (bf16[256,512]{1,0:T(8,128)(2,1)S(1)}, bf16[256,512]{1,0:T(8,128)(2,1)S(1)}, u32[]{:S(2)}, u32[]{:S(2)}) collective-permute-start(bf16[256,512]{1,0:T(8,128)(2,1)S(1)} %pad_maximum_fusion.5), channel_id=1, source_target_pairs={{0,2},{1,3},{2,0},{3,1},{4,6},{5,7},{6,4},{7,5},{8,10},{9,11},{10,... | collective-permute-start | bytes 786440 | tf_op jit(solution)/shard_map/ppermute | solution.py:187
  108.6 14.7 %collective-permute-start.5 = (bf16[128,512]{1,0:T(8,128)(2,1)S(1)}, bf16[128,512]{1,0:T(8,128)(2,1)S(1)}, u32[]{:S(2)}, u32[]{:S(2)}) collective-permute-start(bf16[128,512]{1,0:T(8,128)(2,1)S(1)} %get-tuple-element.6), channel_id=1, source_target_pairs={{0,4},{1,5},{2,6},{3,7},{4,0},{5,1},{6,2},{7,3},{8,12},{9,13},{10,... | collective-permute-start | bytes 393224 | tf_op jit(solution)/shard_map/ppermute | solution.py:187
  117.5 18.0 %collective-permute-start.17 = (bf16[512,512]{1,0:T(8,128)(2,1)S(1)}, bf16[512,512]{1,0:T(8,128)(2,1)S(1)}, u32[]{:S(2)}, u32[]{:S(2)}) collective-permute-start(bf16[512,512]{1,0:T(8,128)(2,1)S(1)} %pad_maximum_fusion.3), channel_id=1, source_target_pairs={{0,16},{1,9},{2,18},{3,11},{4,20},{5,13},{6,22},{7,15},{8,24},{9,1... | collective-permute-start | bytes 1572872 | tf_op jit(solution)/shard_map/ppermute | solution.py:184
  123.3 6.4 %collective-permute-start.6 = (bf16[256,512]{1,0:T(8,128)(2,1)S(1)}, bf16[256,512]{1,0:T(8,128)(2,1)S(1)}, u32[]{:S(2)}, u32[]{:S(2)}) collective-permute-start(bf16[256,512]{1,0:T(8,128)(2,1)S(1)} %pad_maximum_fusion.4), channel_id=1, source_target_pairs={{0,2},{1,3},{2,0},{3,1},{4,6},{5,7},{6,4},{7,5},{8,10},{9,11},{10,... | collective-permute-start | bytes 786440 | tf_op jit(solution)/shard_map/ppermute | solution.py:187
  129.8 17.0 %collective-permute-start.7 = (bf16[512,512]{1,0:T(8,128)(2,1)S(1)}, bf16[512,512]{1,0:T(8,128)(2,1)S(1)}, u32[]{:S(2)}, u32[]{:S(2)}) collective-permute-start(bf16[512,512]{1,0:T(8,128)(2,1)S(1)} %pad_maximum_fusion.2), channel_id=1, source_target_pairs={{0,16},{1,9},{2,18},{3,11},{4,20},{5,13},{6,22},{7,15},{8,24},{9,1... | collective-permute-start | bytes 1572872 | tf_op jit(solution)/shard_map/ppermute | solution.py:184
  135.7 14.9 %collective-permute-start.18 = (bf16[512,1024]{1,0:T(8,128)(2,1)S(1)}, bf16[512,1024]{1,0:T(8,128)(2,1)S(1)}, u32[]{:S(2)}, u32[]{:S(2)}) collective-permute-start(bf16[512,1024]{1,0:T(8,128)(2,1)S(1)} %pad_maximum_fusion.1.a), channel_id=1, source_target_pairs={{0,8},{1,17},{2,10},{3,19},{4,12},{5,21},{6,14},{7,23},{8,0},{9,25... | collective-permute-start | bytes 3145736 | tf_op jit(solution)/shard_map/ppermute | solution.py:184
  146.9 14.9 %collective-permute-start.8 = (bf16[512,1024]{1,0:T(8,128)(2,1)S(1)}, bf16[512,1024]{1,0:T(8,128)(2,1)S(1)}, u32[]{:S(2)}, u32[]{:S(2)}) collective-permute-start(bf16[512,1024]{1,0:T(8,128)(2,1)S(1)} %pad_maximum_fusion.a), channel_id=1, source_target_pairs={{0,8},{1,17},{2,10},{3,19},{4,12},{5,21},{6,14},{7,23},{8,0},{9,25... | collective-permute-start | bytes 3145736 | tf_op jit(solution)/shard_map/ppermute | solution.py:184
  160.0 11.4 %collective-permute-start.19 = (bf16[2048,512]{1,0:T(8,128)(2,1)S(1)}, bf16[2048,512]{1,0:T(8,128)(2,1)S(1)}, u32[]{:S(2)}, u32[]{:S(2)}) collective-permute-start(bf16[2048,512]{1,0:T(8,128)(2,1)S(1)} %mapped.3.m), channel_id=1, source_target_pairs={{0,1},{1,0},{2,3},{3,2},{4,5},{5,4},{6,7},{7,6},{8,9},{9,8},{10,11... | collective-permute-start | bytes 6291464 | tf_op jit(solution)/shard_map/ppermute | solution.py:187
  171.2 12.5 %collective-permute-start.9 = (bf16[2048,512]{1,0:T(8,128)(2,1)S(1)}, bf16[2048,512]{1,0:T(8,128)(2,1)S(1)}, u32[]{:S(2)}, u32[]{:S(2)}) collective-permute-start(bf16[2048,512]{1,0:T(8,128)(2,1)S(1)} %mapped.2.m), channel_id=1, source_target_pairs={{0,1},{1,0},{2,3},{3,2},{4,5},{5,4},{6,7},{7,6},{8,9},{9,8},{10,11... | collective-permute-start | bytes 6291464 | tf_op jit(solution)/shard_map/ppermute | solution.py:187
